TPU v7x, 128 devices: a whole 4x4x4 slice. The times are simulated.
128 devices in a mesh: dp: 8 (over z, x_lo), ctx: 16 (over x_hi, y, core).
Axes of the slice: x: 4 (x_hi: 2, x_lo: 2; x = x_hi * 2 + x_lo), y: 4, z: 4, core: 2. Of those that a mesh axis runs over, the one named last changes fastest.
Arguments:
- tokens: bfloat16 [16384, 1024], P(('dp', 'ctx')), may hold values from -6 to 6
- lengths: int32 [8, 8], P('dp'), may hold values from 1 to 1943, as said below
- attn_gain: bfloat16 [1024], P(('dp', 'ctx')), may hold values from 0.099609375 to 1.8984375
- q_gain: bfloat16 [128], P(('dp', 'ctx')), may hold values from 0.099609375 to 1.8984375
- k_gain: bfloat16 [128], P(('dp', 'ctx')), may hold values from 0.099609375 to 1.8984375
- query_key_value_weight: bfloat16 [1024, 4096], P(('dp', 'ctx')), may hold values from -0.1875 to 0.1875
- w_out: bfloat16 [2048, 1024], P(('dp', 'ctx')), may hold values from -0.75 to 0.75
- mlp_gain: bfloat16 [1024], P(('dp', 'ctx')), may hold values from 0.099609375 to 1.8984375
- w_gate_up: bfloat16 [1024, 6144], P(('dp', 'ctx')), may hold values from -0.1875 to 0.1875
- w_down: bfloat16 [3072, 1024], P(('dp', 'ctx')), may hold values from -0.109375 to 0.109375
- cotangent: bfloat16 [16384, 1024], P(('dp', 'ctx')), may hold values from -6 to 6
Outputs:
- output: float32 [16384, 1024], P(('dp', 'ctx'))
- input_grad: float32 [16384, 1024], P(('dp', 'ctx'))
- grad_attn_gain: float32 [1024], P(('dp', 'ctx'))
- grad_q_gain: float32 [128], P(('dp', 'ctx'))
- grad_k_gain: float32 [128], P(('dp', 'ctx'))
- grad_w_qkv: float32 [1024, 4096], P(('dp', 'ctx'))
- grad_w_out: float32 [2048, 1024], P(('dp', 'ctx'))
- grad_mlp_gain: float32 [1024], P(('dp', 'ctx'))
- grad_gate_up: float32 [1024, 6144], P(('dp', 'ctx'))
- grad_down: float32 [3072, 1024], P(('dp', 'ctx'))
Inputs may be any that keep to these rules, and one draw needn't show every extreme that they name: Row p holds the lengths of the 8 documents of pack p in order; they sum to 2048. The second document of every pack has the largest length.
All inputs are finite; a program needn't handle non-finite values.
Results may differ from a plain program's by a relative error of at most 0.024.
Values may be sent and summed in bfloat16 or wider, within the bound.
A program may use at most 320 MiB of HBM per device.

v0:
```python
import math

import jax
import jax.numpy as jnp
from jax import lax
from jax.sharding import Mesh
from jax.sharding import PartitionSpec as P

QUERY_HEADS = 16
KEY_VALUE_HEADS = 8
HEAD_SIZE = 128
FF = 3072
CTX = ("ctx_0", "ctx_1", "ctx_2")
DP_CTX = ("dp_0", "dp_1", "ctx_0", "ctx_1", "ctx_2")
DP = ("dp_0", "dp_1")


EPS = 1e-06
NEG = -1e30
THETA = 1000000.0


def laid_out(tiles, dim):
    dims = list(tiles.shape[1:])
    dims[dim] *= tiles.shape[0]
    return jnp.moveaxis(tiles, 0, dim).reshape(dims)


def gather_packed(arrays, axis, dims):
    ravelled = jnp.concatenate([a.reshape(-1) for a in arrays])
    lines, at, finished = (lax.all_gather(ravelled, axis), 0, [])
    for a, dim in zip(arrays, dims):
        tiles = lines[:, at : at + a.size].reshape(-1, *a.shape)
        finished.append(laid_out(tiles, dim))
        at += a.size
    return tuple(finished)


def sent_together(arrays, axis, dim, along):
    widths = [a.shape[along] for a in arrays]
    both = jnp.concatenate(arrays, axis=along)
    out = lax.all_gather(both, axis, axis=dim, tiled=True)
    return tuple(jnp.split(out, [sum(widths[:k]) for k in range(1, len(widths))], axis=along))


def in_blocks(shard, dim, peers):
    before, after = (shard.shape[:dim], shard.shape[dim + 1 :])
    return jnp.moveaxis(shard.reshape(*before, peers, -1, *after), dim, 0)


def summed_rows_2(shard, chips, core, dim):
    sizes = (lax.axis_size(chips), lax.axis_size(core))
    tiles = in_blocks(shard, dim, sizes[0] * sizes[1])
    inside = tiles.shape[1:]
    tiles = tiles.reshape(*sizes, *inside).swapaxes(0, 1).reshape(-1, *inside)
    tiles = lax.psum_scatter(tiles, core, scatter_dimension=0, tiled=True)
    return lax.psum_scatter(tiles, chips, scatter_dimension=0, tiled=True)[0]


def scatter_lines(shard, axis, dim):
    peers = lax.axis_size(axis)
    tiles = in_blocks(shard, dim, peers)
    lines = tiles.reshape(peers, -1)
    extent = max(16, -(-lines.shape[1] // 1024) * 8)
    lines = jnp.pad(lines, ((0, 0), (0, extent * 128 - lines.shape[1]))).reshape(-1, 128)
    own = lax.psum_scatter(lines, axis, scatter_dimension=0, tiled=True)
    return own.reshape(-1)[: tiles[0].size].reshape(tiles.shape[1:])


def side_by_side(arrays, axis, dim, along):
    ends, at = ([], 0)
    for a in arrays[:-1]:
        at += a.shape[along]
        ends.append(at)
    both = jnp.concatenate(arrays, axis=along)
    return tuple(
        jnp.split(lax.psum_scatter(both, axis, scatter_dimension=dim, tiled=True), ends, axis=along)
    )


def one_scatter(arrays, axis, dims):
    peers = lax.axis_size(axis)
    tiles = [in_blocks(a, dim, peers) for a, dim in zip(arrays, dims)]
    lines = jnp.concatenate([b.reshape(peers, -1) for b in tiles], axis=1)
    extent = max(16, -(-lines.shape[1] // 1024) * 8)
    lines = jnp.pad(lines, ((0, 0), (0, extent * 128 - lines.shape[1]))).reshape(-1, 128)
    ravelled, at, finished = (lax.psum_scatter(lines, axis, tiled=True).reshape(-1), 0, [])
    for b in tiles:
        part = b[0]
        finished.append(ravelled[at : at + part.size].reshape(part.shape))
        at += part.size
    return tuple(finished)


def layout(doc_lengths, group):
    ends = jnp.cumsum(doc_lengths)
    place = jnp.arange(group, dtype=jnp.int32)
    segment = jnp.sum((place[:, None] >= ends[None, :]).astype(jnp.int32), 1)
    starts = ends - doc_lengths
    picked = segment[:, None] == jnp.arange(doc_lengths.shape[0], dtype=jnp.int32)[None, :]
    begin = jnp.sum(jnp.where(picked, starts[None, :], 0), 1)
    return (segment, place - begin)


def angles(position):
    half_dim = HEAD_SIZE // 2
    freq = THETA ** (-(jnp.arange(half_dim, dtype=jnp.float32) * 2.0 / HEAD_SIZE))
    phase = position.astype(jnp.float32)[:, None] * freq[None, :]
    phase = jnp.concatenate([phase, phase], 1)
    return (jnp.cos(phase), jnp.sin(phase))


def rotate(values_in, cosine, sine):
    half_dim = values_in.shape[-1] // 2
    turned = jnp.concatenate([-values_in[..., half_dim:], values_in[..., :half_dim]], -1)
    return values_in * cosine + turned * sine


def rotate_back(grad_in, cosine, sine):
    half_dim = grad_in.shape[-1] // 2
    scaled = grad_in * sine
    back_part = jnp.concatenate([scaled[..., half_dim:], -scaled[..., :half_dim]], -1)
    return grad_in * cosine + back_part


def norm_back(values_in, inverse, grad_normed):
    cubed = inverse * inverse * inverse
    return inverse * grad_normed - values_in * cubed * jnp.mean(
        grad_normed * values_in, -1, keepdims=True
    )


def contract_rows(left_side, right_side):
    return lax.dot_general(
        left_side, right_side, (((0,), (0,)), ((), ())), preferred_element_type=jnp.float32
    )


def contracted_columns(left_side, right_side):
    return lax.dot_general(
        left_side, right_side, (((1,), (1,)), ((), ())), preferred_element_type=jnp.float32
    )


def on_device(
    tokens,
    lengths,
    attn_gain,
    q_gain,
    k_gain,
    query_key_value_weight,
    w_out,
    mlp_gain,
    w_gate_up,
    w_down,
    cotangent,
):
    local_rows = tokens.shape[0]
    group = local_rows * lax.axis_size(CTX)
    head_groups = QUERY_HEADS // KEY_VALUE_HEADS
    scale_factor = 1.0 / math.sqrt(HEAD_SIZE)
    attn_full = gather_packed(
        (query_key_value_weight, w_out, attn_gain, q_gain, k_gain), DP_CTX, (0, 0, 0, 0, 0)
    )
    mlp_full = gather_packed((w_gate_up, w_down, mlp_gain), DP_CTX, (0, 0, 0))
    qkv_full, out_full, gain_one, gain_query, gain_key = attn_full
    gate_up_full, down_full, gain_two = mlp_full
    inputs = tokens.astype(jnp.float32)
    inverse_one = lax.rsqrt(jnp.mean(inputs * inputs, -1, keepdims=True) + EPS)
    normed_one = inputs * inverse_one
    first_in = (normed_one * gain_one.astype(jnp.float32)).astype(jnp.bfloat16)
    projected_rows = jnp.dot(first_in, qkv_full, preferred_element_type=jnp.float32)
    query_unnormed = projected_rows[:, : QUERY_HEADS * HEAD_SIZE].reshape(
        local_rows, KEY_VALUE_HEADS, head_groups, HEAD_SIZE
    )
    key_unnormed = projected_rows[
        :, QUERY_HEADS * HEAD_SIZE : (QUERY_HEADS + KEY_VALUE_HEADS) * HEAD_SIZE
    ].reshape(local_rows, KEY_VALUE_HEADS, HEAD_SIZE)
    value_reduced = (
        projected_rows[:, (QUERY_HEADS + KEY_VALUE_HEADS) * HEAD_SIZE :]
        .reshape(local_rows, KEY_VALUE_HEADS, HEAD_SIZE)
        .astype(jnp.bfloat16)
    )
    query_inv = lax.rsqrt(jnp.mean(query_unnormed * query_unnormed, -1, keepdims=True) + EPS)
    key_inv = lax.rsqrt(jnp.mean(key_unnormed * key_unnormed, -1, keepdims=True) + EPS)
    query_hat = query_unnormed * query_inv
    key_hat = key_unnormed * key_inv
    query_scale = gain_query.astype(jnp.float32)
    key_scale = gain_key.astype(jnp.float32)
    segment, position = layout(lengths[0], group)
    offset = lax.axis_index(CTX) * local_rows
    my_segment = lax.dynamic_slice_in_dim(segment, offset, local_rows)
    my_position = lax.dynamic_slice_in_dim(position, offset, local_rows)
    my_place = offset + jnp.arange(local_rows, dtype=jnp.int32)
    place = jnp.arange(group, dtype=jnp.int32)
    cosine, sine = angles(my_position)
    cos_query, sin_query = (cosine[:, None, None, :], sine[:, None, None, :])
    cos_key, sin_key = (cosine[:, None, :], sine[:, None, :])
    query_low = rotate(query_hat * query_scale, cos_query, sin_query).astype(jnp.bfloat16)
    key_low = rotate(key_hat * key_scale, cos_key, sin_key).astype(jnp.bfloat16)
    key_all, value_all = sent_together((key_low, value_reduced), CTX, 0, 1)
    visible = (my_segment[:, None] == segment[None, :]) & (my_place[:, None] >= place[None, :])
    scores = (
        jnp.einsum("tkgd,nkd->kgtn", query_low, key_all, preferred_element_type=jnp.float32)
        * scale_factor
    )
    scores = jnp.where(visible, scores, NEG)
    top_score = jnp.max(scores, -1, keepdims=True)
    expd = jnp.exp(scores - top_score)
    total = jnp.sum(expd, -1, keepdims=True)
    probs = expd / total
    log_total = top_score + jnp.log(total)
    attended = jnp.einsum(
        "kgtn,nkd->tkgd", probs.astype(jnp.bfloat16), value_all, preferred_element_type=jnp.float32
    )
    attended_low = attended.reshape(local_rows, QUERY_HEADS * HEAD_SIZE).astype(jnp.bfloat16)
    residual = inputs + jnp.dot(attended_low, out_full, preferred_element_type=jnp.float32)
    inverse_two = lax.rsqrt(jnp.mean(residual * residual, -1, keepdims=True) + EPS)
    normed_two = residual * inverse_two
    second_in = (normed_two * gain_two.astype(jnp.float32)).astype(jnp.bfloat16)
    gate_up = jnp.dot(second_in, gate_up_full, preferred_element_type=jnp.float32)
    gate_part = gate_up[:, :FF]
    up_part = gate_up[:, FF:]
    sigma = jax.nn.sigmoid(gate_part)
    swish = gate_part * sigma
    hidden_low = (swish * up_part).astype(jnp.bfloat16)
    output = residual + jnp.dot(hidden_low, down_full, preferred_element_type=jnp.float32)
    gate_up_back, down_back, gain_two_back = (gate_up_full, down_full, gain_two)
    piece = hidden_low
    grad_down = summed_rows_2(
        contract_rows(piece, cotangent), ("dp_0", "dp_1", "ctx_0", "ctx_1"), "ctx_2", 0
    )
    grad_hidden = contracted_columns(cotangent, down_back)
    grad_gate = grad_hidden * up_part * sigma * (1.0 + gate_part * (1.0 - sigma))
    grad_up = grad_hidden * swish
    grad_gu_low = jnp.concatenate([grad_gate, grad_up], 1).astype(jnp.bfloat16)
    piece = second_in
    grad_gate_up = scatter_lines(contract_rows(piece, grad_gu_low), DP_CTX, 0)
    grad_second = contracted_columns(grad_gu_low, gate_up_back)
    grad_gain_two = jnp.sum(grad_second * normed_two, 0)
    grad_resid = cotangent.astype(jnp.float32) + norm_back(
        residual, inverse_two, grad_second * gain_two_back.astype(jnp.float32)
    )
    residual_reduced = grad_resid.astype(jnp.bfloat16)
    qkv_back, output_backward, gain_one_back, query_gain_back, key_gain_back = (
        qkv_full,
        out_full,
        gain_one,
        gain_query,
        gain_key,
    )
    grad_w_out_term = contract_rows(attended_low, residual_reduced)
    grad_att_low = (
        contracted_columns(residual_reduced, output_backward)
        .astype(jnp.bfloat16)
        .reshape(local_rows, KEY_VALUE_HEADS, head_groups, HEAD_SIZE)
    )
    scores_back = (
        jnp.einsum("tkgd,nkd->kgtn", query_low, key_all, preferred_element_type=jnp.float32)
        * scale_factor
    )
    scores_back = jnp.where(visible, scores_back, NEG)
    probs_back = jnp.exp(scores_back - log_total)
    grad_probs = jnp.einsum(
        "tkgd,nkd->kgtn", grad_att_low, value_all, preferred_element_type=jnp.float32
    )
    inner = jnp.sum(probs_back * grad_probs, -1, keepdims=True)
    grad_scores = (probs_back * (grad_probs - inner)).astype(jnp.bfloat16)
    grad_query = (
        jnp.einsum("kgtn,nkd->tkgd", grad_scores, key_all, preferred_element_type=jnp.float32)
        * scale_factor
    )
    key_term = (
        jnp.einsum("kgtn,tkgd->nkd", grad_scores, query_low, preferred_element_type=jnp.float32)
        * scale_factor
    )
    value_term = jnp.einsum(
        "kgtn,tkgd->nkd",
        probs_back.astype(jnp.bfloat16),
        grad_att_low,
        preferred_element_type=jnp.float32,
    )
    grad_key, value_gradient = side_by_side((key_term, value_term), CTX, 0, 1)
    query_scale_back = query_gain_back.astype(jnp.float32)
    key_scale_back = key_gain_back.astype(jnp.float32)
    grad_query_normed = rotate_back(grad_query, cos_query, sin_query)
    grad_key_normed = rotate_back(grad_key, cos_key, sin_key)
    grad_gain_query = jnp.sum(grad_query_normed * query_hat, (0, 1, 2))
    grad_gain_key = jnp.sum(grad_key_normed * key_hat, (0, 1))
    grad_query_raw = norm_back(query_unnormed, query_inv, grad_query_normed * query_scale_back)
    gradient_key_unnormed = norm_back(key_unnormed, key_inv, grad_key_normed * key_scale_back)
    grad_proj_low = jnp.concatenate(
        [
            grad_query_raw.reshape(local_rows, QUERY_HEADS * HEAD_SIZE),
            gradient_key_unnormed.reshape(local_rows, KEY_VALUE_HEADS * HEAD_SIZE),
            value_gradient.reshape(local_rows, KEY_VALUE_HEADS * HEAD_SIZE),
        ],
        1,
    ).astype(jnp.bfloat16)
    grad_qkv_term = contract_rows(first_in, grad_proj_low)
    grad_first = contracted_columns(grad_proj_low, qkv_back)
    grad_gain_one = jnp.sum(grad_first * normed_one, 0)
    input_grad = grad_resid + norm_back(
        inputs, inverse_one, grad_first * gain_one_back.astype(jnp.float32)
    )
    summed = one_scatter(
        (
            grad_qkv_term,
            grad_w_out_term,
            grad_gain_one,
            grad_gain_query,
            grad_gain_key,
            grad_gain_two,
        ),
        DP_CTX,
        (0, 0, 0, 0, 0, 0),
    )
    grad_w_qkv, grad_w_out, grad_attn_gain, grad_q_gain, grad_k_gain, grad_mlp_gain = summed
    return (
        output,
        input_grad,
        grad_attn_gain,
        grad_q_gain,
        grad_k_gain,
        grad_w_qkv,
        grad_w_out,
        grad_mlp_gain,
        grad_gate_up,
        grad_down,
    )


def solution(mesh):
    torus = Mesh(mesh.devices.reshape(4, 2, 2, 4, 2), ("dp_0", "dp_1", "ctx_0", "ctx_1", "ctx_2"))
    placed = (
        P(DP_CTX, None),
        P(DP, None),
        P(DP_CTX),
        P(DP_CTX),
        P(DP_CTX),
        P(DP_CTX, None),
        P(DP_CTX, None),
        P(DP_CTX),
        P(DP_CTX, None),
        P(DP_CTX, None),
        P(DP_CTX, None),
    )
    return jax.shard_map(
        on_device,
        mesh=torus,
        in_specs=placed,
        out_specs=(
            P(DP_CTX, None),
            P(DP_CTX, None),
            P(DP_CTX),
            P(DP_CTX),
            P(DP_CTX),
            P(DP_CTX, None),
            P(DP_CTX, None),
            P(DP_CTX),
            P(DP_CTX, None),
            P(DP_CTX, None),
        ),
        check_vma=False,
    )
```

profile of v0, /device:TPU:0, one launch (start us, length us, event | category | flops | bytes accessed | tf_op | source)
XLA Modules:
  0.0 2112.6 jit_solution(3486862809121119238)
XLA Ops:
  13.4 4.6 broadcast.184
  18.0 2.9 dynamic-update-slice
  20.9 6.6 broadcast.185
  27.5 3.2 dynamic-update-slice.1
  33.5 284.7 %all-reduce.10.cloned.1.call-done = (bf16[6292736]{0:T(1024)(128)(2,1)}, bf16[9438208]{0:T(1024)(128)(2,1)}) async-done(((bf16[6292736]{0:T(1024)(128)(2,1)}, bf16[9438208]{0:T(1024)(128)(2,1)}), (bf16[6292736]{0:T(1024)(128)(2,1)}, bf16[9438208]{0:T(1024)(128)(2,1)})) %all-reduce.10.cloned.1.call-update) | async-done | bytes 31461904
  318.3 31.4 %reshape.358 = bf16[128,49162]{1,0:T(8,128)(2,1)} reshape(bf16[6292736]{0:T(1024)(128)(2,1)} %get-tuple-element.20) | data formatting | bytes 25170944 | tf_op jit(solution)/shard_map/all_gather | solution.py:31
  351.5 7.5 slice.112
  359.1 13.5 reshape_reshape.25
  372.6 4.7 fusion.46
  383.4 4.6 slice.122
  387.9 44.5 %reshape.359 = bf16[128,73736]{1,0:T(8,128)(2,1)} reshape(bf16[9438208]{0:T(1024)(128)(2,1)} %get-tuple-element.21) | data formatting | bytes 37752832 | tf_op jit(solution)/shard_map/all_gather | solution.py:31
  432.4 5.9 slice.127
  438.4 10.6 slice.124
  449.0 7.6 reshape_reshape.26
  460.3 17.1 reshape_reshape.27
  477.4 8.9 reshape_reshape.28
  487.0 10.5 fusion.61
  497.5 8.2 fusion.3
  505.7 11.3 fusion.17
  517.0 3.3 multiply_reduce_fusion.6
  522.3 4.2 multiply_convert_fusion.1
  526.5 6.6 multiply_reduce_fusion.3
  534.6 3.7 convolution_convert_fusion
  538.6 8.1 fusion.10
  546.7 11.9 fusion
  558.6 12.2 fusion.2
  570.8 2.3 fusion.7
  574.1 6.1 pad_maximum_fusion
  581.5 6.8 fusion.62
  588.2 16.3 copy.238
  605.9 4.5 fusion.42
  610.4 9.5 reshape_reshape.30
  619.9 6.7 broadcast_multiply_fusion
  628.2 2.3 subtract_convert_fusion
  630.5 95.1 %reduce-scatter.5.cloned.1.call-done = f32[128,16,128]{2,0,1:T(8,128)} async-done(((f32[2048,16,128]{2,0,1:T(8,128)}), f32[128,16,128]{2,0,1:T(8,128)}) %reduce-scatter.5.cloned.1.call-update) | async-done | bytes 1048592 | tf_op jit(solution)/shard_map/reduce_scatter | solution.py:77
  730.5 7.1 fusion.26
  737.8 11.3 fusion.39
  749.1 18.4 reshape_reshape.29
  767.4 11.2 constant_dynamic-update-slice_fusion.1
  778.7 7.4 constant_dynamic-update-slice_fusion
  792.4 17.0 pad.4
  809.4 23.5 %reshape.348 = f32[50176,128]{1,0:T(8,128)} reshape(f32[128,50176]{1,0:T(8,128)} %pad.4) | data formatting | bytes 51380224 | tf_op jit(solution)/shard_map/reshape | solution.py:86
  834.5 11.4 fusion.21
  845.8 26.6 %reshape.352 = f32[49152,128]{1,0:T(8,128)} reshape(f32[1024,6144]{1,0:T(8,128)} %fusion.21) | data formatting | bytes 50331648 | tf_op jit(solution)/shard_map/reshape | solution.py:65
  873.8 5.6 convolution_add_fusion.1
  880.4 184.4 %all-reduce.8.cloned.1.call-done = f32[50176,128]{1,0:T(8,128)} async-done(((f32[50176,128]{1,0:T(8,128)}), f32[50176,128]{1,0:T(8,128)}) %all-reduce.8.cloned.1.call-update) | async-done | bytes 25690128
  1070.1 675.1 %reduce-scatter.7.cloned.1.call-done = f32[384,128]{1,0:T(8,128)} async-done(((f32[49152,128]{1,0:T(8,128)}), f32[384,128]{1,0:T(8,128)}) %reduce-scatter.7.cloned.1.call-update) | async-done | bytes 196624 | tf_op jit(solution)/shard_map/reduce_scatter | solution.py:66
  1746.9 358.6 %reduce-scatter.11.cloned.1.call-done = f32[1,24,1024]{2,1,0:T(8,128)} async-done(((f32[64,24,1024]{2,1,0:T(8,128)}), f32[1,24,1024]{2,1,0:T(8,128)}) %reduce-scatter.11.cloned.1.call-update) | async-done | bytes 98320 | tf_op jit(solution)/shard_map/reduce_scatter | solution.py:57
  (196 shorter events, 50.2 us)
Async XLA Ops:
  7.2 311.1 %all-reduce.10.cloned.1.call-start = ((), (), s32[]{:S(2)}) async-start(), calls=%async_computation.10 | async-start | bytes 62926848
  30.7 2.2 copy-start.7
  30.7 456.3 %all-gather.4.cloned.1.call-start = ((), (), s32[]{:S(2)}) async-start(), calls=%async_computation.4 | async-start | bytes 8912896 | tf_op jit(solution)/shard_map/all_gather | solution.py:42
  32.9 349.2 %copy-start.21 = (f32[128,128]{1,0:T(8,128)}, f32[128,128]{1,0:T(8,128)S(1)}, u32[]{:S(2)}) copy-start(f32[128,128]{1,0:T(8,128)S(1)} %get-tuple-element.43) | copy-start | bytes 196612
  32.9 349.3 %copy-start.19 = (f32[128,128]{1,0:T(8,128)}, f32[128,128]{1,0:T(8,128)S(1)}, u32[]{:S(2)}) copy-start(f32[128,128]{1,0:T(8,128)S(1)} %get-tuple-element.44) | copy-start | bytes 196612
  33.5 339.0 %copy-start.34 = (f32[128]{0:T(128)}, f32[128]{0:T(128)S(1)}, u32[]{:S(2)}) copy-start(f32[128]{0:T(128)S(1)} %get-tuple-element.50) | copy-start | bytes 1540
  350.7 28.9 %copy-start.37 = (f32[128]{0:T(128)}, f32[128]{0:T(128)S(1)}, u32[]{:S(2)}) copy-start(f32[128]{0:T(128)S(1)} %get-tuple-element.10) | copy-start | bytes 1540
  359.1 13.5 copy-start.25
  377.3 10.6 copy-start.8
  378.2 9.7 copy-start.5
  379.2 8.7 copy-start.30
  381.8 343.8 %reduce-scatter.5.cloned.1.call-start = ((), (), s32[]{:S(2)}) async-start(), calls=%async_computation.5 | async-start | bytes 17825792 | tf_op jit(solution)/shard_map/reduce_scatter | solution.py:77
  449.0 7.6 slice-start.5
  458.0 28.7 %copy-start.1 = (f32[128,8,2,128]{0,3,2,1:T(8,128)}, f32[128,8,2,128]{0,3,2,1:T(8,128)S(1)}, u32[]{:S(2)}) copy-start(f32[128,8,2,128]{0,3,2,1:T(8,128)S(1)} %copy.210) | copy-start | bytes 3145732
  460.3 72.9 %copy-start.23 = (f32[1024]{0:T(1024)}, f32[1024]{0:T(1024)S(1)}, u32[]{:S(2)}) copy-start(f32[1024]{0:T(1024)S(1)} %reshape.357) | copy-start | bytes 12292
  486.9 10.6 copy-start.14
  497.5 22.8 %slice-start = ((s8[12582912]{0:T(1024)(128)(4,1)}), s8[4194304]{0:T(1024)(128)(4,1)S(1)}, s32[]{:S(2)}) async-start(s8[12582912]{0:T(1024)(128)(4,1)} %bitcast.136), calls=%async_computation.11 | async-start | bytes 8388608
  505.7 14.7 slice-start.1
  505.7 14.7 slice-start.2
  517.0 5.3 slice-start.3
  520.3 2.0 copy-start.3
  520.3 12.8 copy-start.32
  520.4 1.9 slice-start.4
  520.4 1.9 copy-start.17
  558.6 12.2 copy-start.15
  570.8 3.4 copy-start
  580.3 292.3 %reduce-scatter.9.cloned.1.call-start = ((), (), s32[]{:S(2)}) async-start(), calls=%async_computation.7 | async-start | bytes 18874368 | tf_op jit(solution)/shard_map/reduce_scatter | solution.py:56
  604.6 1.3 copy-start.11
  604.6 460.3 %all-reduce.8.cloned.1.call-start = ((), (), s32[]{:S(2)}) async-start(), calls=%async_computation.9 | async-start | bytes 51380224
  619.9 6.9 copy-start.2
  626.6 100.2 %copy-start.22 = (f32[128,128]{1,0:T(8,128)S(1)}, f32[128,128]{1,0:T(8,128)}, u32[]{:S(2)}) copy-start(f32[128,128]{1,0:T(8,128)} %copy-done.21) | copy-start | bytes 196612
  626.7 101.5 %copy-start.6 = (f32[16,8,8,128]{3,2,1,0:T(8,128)S(1)}, f32[16,8,8,128]{3,2,1,0:T(8,128)}, u32[]{:S(2)}) copy-start(f32[16,8,8,128]{3,2,1,0:T(8,128)} %copy-done.5) | copy-start | bytes 1572868
  626.7 101.5 %copy-start.20 = (f32[128,128]{1,0:T(8,128)S(1)}, f32[128,128]{1,0:T(8,128)}, u32[]{:S(2)}) copy-start(f32[128,128]{1,0:T(8,128)} %copy-done.19) | copy-start | bytes 196612
  626.7 101.5 %copy-start.31 = (f32[128,8]{0,1:T(8,128)S(1)}, f32[128,8]{0,1:T(8,128)}, u32[]{:S(2)}) copy-start(f32[128,8]{0,1:T(8,128)} %copy-done.30) | copy-start | bytes 12292
  626.7 101.5 %copy-start.38 = (f32[128]{0:T(128)S(1)}, f32[128]{0:T(128)}, u32[]{:S(2)}) copy-start(f32[128]{0:T(128)} %copy-done.37) | copy-start | bytes 1540
  626.7 103.1 %copy-start.36 = (f32[128,8]{0,1:T(8,128)S(1)}, f32[128,8]{0,1:T(8,128)}, u32[]{:S(2)}) copy-start(f32[128,8]{0,1:T(8,128)} %get-tuple-element.47) | copy-start | bytes 12292
  626.8 103.7 %copy-start.26 = (f32[1024]{0:T(1024)S(1)}, f32[1024]{0:T(1024)}, u32[]{:S(2)}) copy-start(f32[1024]{0:T(1024)} %copy-done.25) | copy-start | bytes 12292
  626.8 103.7 %copy-start.35 = (f32[128]{0:T(128)S(1)}, f32[128]{0:T(128)}, u32[]{:S(2)}) copy-start(f32[128]{0:T(128)} %copy-done.34) | copy-start | bytes 1540
  630.5 100.0 %copy-start.16 = (bf16[128,8,2,128]{0,3,2,1:T(8,128)(2,1)S(1)}, bf16[128,8,2,128]{0,3,2,1:T(8,128)(2,1)}, u32[]{:S(2)}) copy-start(bf16[128,8,2,128]{0,3,2,1:T(8,128)(2,1)} %subtract_convert_fusion) | copy-start | bytes 1572868
  832.9 1.3 copy-start.12
  832.9 1.5 copy-start.13
  832.9 1.5 copy-start.24
  832.9 1.5 copy-start.33
  833.0 912.3 %reduce-scatter.7.cloned.1.call-start = ((), (), s32[]{:S(2)}) async-start(), calls=%async_computation.6 | async-start | bytes 25362432 | tf_op jit(solution)/shard_map/reduce_scatter | solution.py:66
  872.5 1.3 copy-start.10
  872.5 6.9 copy-start.27
  872.5 6.9 copy-start.39
  872.5 1232.9 %reduce-scatter.11.cloned.1.call-start = ((), (), s32[]{:S(2)}) async-start(), calls=%async_computation.8 | async-start | bytes 6389760 | tf_op jit(solution)/shard_map/reduce_scatter | solution.py:57
  (6 other events, 5.8 us)
Sparse Core Ops, SparseCore 0:
  30.8 287.4 all-reduce.9
  381.9 70.9 all-gather.3
  580.4 145.1 reduce-scatter.4
  728.0 21.9 reduce-scatter.8
  833.1 231.7 all-reduce.7
  1067.1 678.0 reduce-scatter.6
  1748.2 357.2 reduce-scatter.10
where the time goes:
time: 2130 us; the launch traced here: 2110 us
  waiting for transfers between devices  1600 us (75%)
  local copies, waits for them, and re-layouts  327 us (15%)
  matrix products  122 us (6%)
  other arithmetic  47.5 us (2%)
    reduce_scatter x1, waiting for transfers between devices, scatter_lines(): own = lax.psum_scatter(lines, axis, scatter_dimension=0, tiled=True)  675 us
    unnamed x9, waiting for transfers between devices  470 us
    reduce_scatter x1, waiting for transfers between devices, summed_rows_2(): return lax.psum_scatter(tiles, chips, scatter_dimension=0, tiled=True)[0]  359 us
    reduce_scatter x1, waiting for transfers between devices, side_by_side(): lax.psum_scatter(both, axis, scatter_dimension=dim, tiled=True)  95.1 us
    all_gather x2, local copies, waits for them, and re-layouts, gather_packed(): lines, at, finished = (lax.all_gather(ravelled, axis), 0, [])  75.9 us
    unnamed x107, local copies, waits for them, and re-layouts  49.9 us
    another operation x4, local copies, waits for them, and re-layouts, laid_out(): return jnp.moveaxis(tiles, 0, dim).reshape(dims)  47.2 us
  transfers between devices with their start and end apart: 7, of which 5 were waited for; matrix products, arithmetic and copies ran while one was open for 15% of the time, Pallas kernels for 0%

commit v1 on v0

v1 whole, which is shorter than its diff:
```python
import functools
import math

import jax
import jax.numpy as jnp
from jax import lax
from jax.experimental import pallas as pl
from jax.experimental.pallas import tpu as pltpu
from jax.sharding import Mesh
from jax.sharding import PartitionSpec as P

QUERY_HEADS = 16
KEY_VALUE_HEADS = 8
HEAD_SIZE = 128
WIDTH = 1024
FF = 3072
TOK = 128
GROUP = 2048
BLOCK = 256
SLICE = FF // 8
EPS = 1e-06
THETA = 1000000.0
SCALE = 1.0 / math.sqrt(HEAD_SIZE)
SCALE2 = SCALE / math.log(2.0)

AXES = ("z", "xl", "xh", "y", "c")
SIZES = (4, 2, 2, 4, 2)
CTX = ("xh", "y", "c")
DP = ("z", "xl")
BF = jnp.bfloat16
F32 = jnp.float32
BY_MESH = pl.DeviceIdType.MESH
ANY = pl.BlockSpec(memory_space=pl.ANY)
VMEM = pl.BlockSpec(memory_space=pltpu.VMEM)
MIB = 2**20


def offsets(*axes):
    out = [()]
    for size, name in zip(SIZES, AXES):
        out = [o + (k,) for o in out for k in (range(size) if name in axes else (0,))]
    return out[1:]


SIBLING = (0, 0, 0, 0, 1)
CTX_ALL = offsets("xh", "y", "c")
CTX_SAME = offsets("xh", "y")
DP_ALL = offsets("z", "xl")
PLANE = offsets("xl", "xh", "y")
RING = offsets("z")
RING_ALL = offsets("z", "c")


def place():
    return tuple(lax.axis_index(a) for a in AXES)


def moved(me, offset):
    return tuple(lax.rem(m + o, s) if o else m for m, o, s in zip(me, offset, SIZES))


def before(me, offset):
    return tuple(lax.rem(m + s - o, s) if o else m for m, o, s in zip(me, offset, SIZES))


def ctx_of(at):
    return at[2] * 8 + at[3] * 2 + at[4]


def dp_of(at):
    return at[0] * 2 + at[1]


def ring_of(at):
    return at[0] * 2 + at[4]


def plane_of(at):
    return at[1] * 8 + at[2] * 4 + at[3]


def greet(me, peers):
    barrier = pltpu.get_barrier_semaphore()
    for o in peers:
        pl.semaphore_signal(barrier, inc=1, device_id=moved(me, o), device_id_type=BY_MESH)
    pl.semaphore_wait(barrier, len(peers))


class Net:
    def __init__(self, send, recv):
        self.send, self.recv, self.count, self.sent = send, recv, 0, []

    def put(self, src, dst, device):
        k = self.count
        self.count += 1
        copy = pltpu.make_async_remote_copy(
            src_ref=src,
            dst_ref=dst,
            send_sem=self.send.at[k],
            recv_sem=self.recv.at[k],
            device_id=device,
            device_id_type=BY_MESH,
        )
        copy.start()
        self.sent.append(copy)
        return copy

    def local(self, src, dst):
        k = self.count
        self.count += 1
        copy = pltpu.make_async_copy(src, dst, self.send.at[k])
        copy.start()
        return copy

    def finish(self):
        for copy in self.sent:
            copy.wait_send()


def sems(count):
    return [pltpu.SemaphoreType.DMA((count,)), pltpu.SemaphoreType.DMA((count,))]


def remote(body, name, identity, outs, ins, out_specs, scratch, *operands):
    return pl.pallas_call(
        body,
        name=name,
        out_shape=outs,
        in_specs=ins,
        out_specs=out_specs,
        scratch_shapes=scratch,
        compiler_params=pltpu.CompilerParams(
            collective_id=identity, has_side_effects=True, vmem_limit_bytes=50 * MIB
        ),
    )(*operands)


def shape(dims, kind):
    return jax.ShapeDtypeStruct(dims, kind)


def first_gather_body(tok, wq, gains, x_out, w_out, g_out, w_tmp, w_low, g_tmp, g_row, send, recv):
    me = place()
    net = Net(send, recv)
    greet(me, CTX_ALL + DP_ALL)
    mine = ctx_of(me)
    small, rows = [], []
    for o in CTX_ALL:
        to = moved(me, o)
        small.append(net.put(wq.at[ctx_of(to)], w_tmp.at[mine], to))
        small.append(net.put(gains, g_tmp.at[mine], to))
    for o in CTX_SAME:
        rows.append(net.put(tok, x_out.at[mine], moved(me, o)))
    over = moved(me, SIBLING)
    passed = [net.put(tok, x_out.at[mine], over)]
    locals_ = [
        net.local(wq.at[mine], w_tmp.at[mine]),
        net.local(gains, g_tmp.at[mine]),
        net.local(tok, x_out.at[mine]),
    ]
    for copy in locals_[:2]:
        copy.wait()
    for copy in small:
        copy.wait_recv()
    w_low[...] = w_tmp[...].reshape(TOK, 3 * HEAD_SIZE).astype(BF)
    g_row[...] = g_tmp[:, 0, :]
    here = dp_of(me)
    wide = []
    for o in DP_ALL:
        to = moved(me, o)
        wide.append(net.put(w_low, w_out.at[here], to))
        wide.append(net.put(g_row, g_out.at[here], to))
    more = [net.local(w_low, w_out.at[here]), net.local(g_row, g_out.at[here])]
    for o, copy in zip(CTX_SAME, rows):
        copy.wait_recv()
        source = ctx_of(before(me, o))
        passed.append(net.put(x_out.at[source], x_out.at[source], over))
    for copy in wide + passed:
        copy.wait_recv()
    locals_[2].wait()
    for copy in more:
        copy.wait()
    net.finish()


def first_gather(tokens, wq, gains):
    return remote(
        first_gather_body,
        "first_gather",
        1,
        (shape((16, TOK, WIDTH), BF), shape((8, TOK, 3 * HEAD_SIZE), BF), shape((8, 16, 128), F32)),
        [ANY, ANY, ANY],
        (ANY, ANY, ANY),
        [
            pltpu.VMEM((16, 8, 3 * HEAD_SIZE), F32),
            pltpu.VMEM((TOK, 3 * HEAD_SIZE), BF),
            pltpu.VMEM((16, 8, 128), F32),
            pltpu.VMEM((16, 128), F32),
        ]
        + sems(72),
        tokens,
        wq,
        gains,
    )


def swapped(me, offset):
    at = moved(me, offset)
    return (at[0], at[4], at[2], at[3], at[1])


def weight_gather_body(
    wo, wgu, wd, cot, wo_out, gu_out, wd_out, cot_out, gu_tmp, gu_low, wd_tmp, wd_low, send, recv, gate
):
    me = place()
    z, xl, xh, y, c = me
    net = Net(send, recv)
    barrier = pltpu.get_barrier_semaphore()
    peers = PLANE + RING_ALL
    for o in peers:
        pl.semaphore_signal(barrier, inc=1, device_id=moved(me, o), device_id_type=BY_MESH)
    for o in CTX_SAME:
        pl.semaphore_signal(barrier, inc=1, device_id=swapped(me, o), device_id_type=BY_MESH)

    @pl.when(xl != c)
    def _():
        pl.semaphore_signal(barrier, inc=1, device_id=(z, c, xh, y, xl), device_id_type=BY_MESH)

    pl.semaphore_wait(barrier, len(peers) + len(CTX_SAME) + (xl + c - 2 * xl * c))
    over = moved(me, SIBLING)
    down = net.put(wd, wd_tmp.at[c], over)
    slices = []
    for o in RING_ALL:
        to = moved(me, o)
        slices.append(net.put(wgu.at[ring_of(to)], gu_tmp.at[ring_of(me)], to))
    own = [
        net.local(wd, wd_tmp.at[c]),
        net.local(wgu.at[ring_of(me)], gu_tmp.at[ring_of(me)]),
        net.local(wo, wo_out.at[z, xl, xh, y, c]),
        net.local(cot, cot_out.at[z, c]),
    ]
    outs = [net.put(wo, wo_out.at[z, xl, xh, y, c], moved(me, o)) for o in PLANE]
    cots = [net.put(cot, cot_out.at[z, c], moved(me, o)) for o in RING]
    passed = [net.put(cot, cot_out.at[z, c], over)]
    own[0].wait()
    down.wait_recv()
    wd_low[...] = wd_tmp[...].reshape(48, WIDTH).astype(BF)
    downs = [net.put(wd_low, wd_out.at[xh, y], swapped(me, o)) for o in CTX_SAME]

    @pl.when(xl != c)
    def _():
        copy = pltpu.make_async_remote_copy(
            src_ref=wd_low,
            dst_ref=wd_out.at[xh, y],
            send_sem=gate.at[0],
            recv_sem=gate.at[1],
            device_id=(z, c, xh, y, xl),
            device_id_type=BY_MESH,
        )
        copy.start()
        copy.wait()

    @pl.when(xl == c)
    def _():
        copy = pltpu.make_async_copy(wd_low, wd_out.at[xh, y], gate.at[0])
        copy.start()
        copy.wait()

    own[1].wait()
    for copy in slices:
        copy.wait_recv()
    gu_low[...] = gu_tmp[...].reshape(4, 16, 2 * SLICE).astype(BF)
    ups = [net.put(gu_low, gu_out.at[:, xl, xh, y], moved(me, o)) for o in PLANE]
    own.append(net.local(gu_low, gu_out.at[:, xl, xh, y]))
    own[2].wait()
    for copy in outs:
        copy.wait_recv()
    wide = [net.put(wo_out.at[z, :, :, :, c], wo_out.at[z, :, :, :, c], moved(me, o)) for o in RING]
    passed.append(net.put(wo_out.at[z, :, :, :, c], wo_out.at[z, :, :, :, c], over))
    for o, copy in zip(RING, cots):
        copy.wait_recv()
        s = before(me, o)[0]
        passed.append(net.put(cot_out.at[s, c], cot_out.at[s, c], over))
    for o, copy in zip(RING, wide):
        copy.wait_recv()
        s = before(me, o)[0]
        passed.append(net.put(wo_out.at[s, :, :, :, c], wo_out.at[s, :, :, :, c], over))
    for copy in downs + ups + passed:
        copy.wait_recv()
    for copy in own[3:]:
        copy.wait()
    net.finish()


def weight_gather(wo, wgu, wd, cot):
    return remote(
        weight_gather_body,
        "weight_gather",
        2,
        (
            shape((4, 2, 2, 4, 2, 16, WIDTH), BF),
            shape((4, 2, 2, 4, 16, 2 * SLICE), BF),
            shape((2, 4, 48, WIDTH), BF),
            shape((4, 2, TOK, WIDTH), BF),
        ),
        [ANY] * 4,
        (ANY,) * 4,
        [
            pltpu.VMEM((8, 8, 2 * SLICE), F32),
            pltpu.VMEM((4, 16, 2 * SLICE), BF),
            pltpu.VMEM((2, 24, WIDTH), F32),
            pltpu.VMEM((48, WIDTH), BF),
        ]
        + sems(72)
        + [pltpu.SemaphoreType.DMA((2,))],
        wo,
        wgu,
        wd,
        cot,
    )


def heads_to_tokens_body(src, dst, send, recv):
    me = place()
    net = Net(send, recv)
    greet(me, CTX_ALL)
    mine = ctx_of(me)
    columns = pl.ds(pl.multiple_of(mine * HEAD_SIZE, HEAD_SIZE), HEAD_SIZE)
    copies = []
    for o in CTX_ALL:
        to = moved(me, o)
        copies.append(net.put(src.at[ctx_of(to)], dst.at[:, columns], to))
    own = net.local(src.at[mine], dst.at[:, columns])
    for copy in copies:
        copy.wait_recv()
    own.wait()
    net.finish()


def heads_to_tokens(attended):
    return remote(
        heads_to_tokens_body,
        "heads_to_tokens",
        3,
        shape((TOK, QUERY_HEADS * HEAD_SIZE), BF),
        [ANY],
        ANY,
        sems(16),
        attended.reshape(16, TOK, HEAD_SIZE),
    )


def tokens_to_heads_body(src, dst, send, recv):
    me = place()
    net = Net(send, recv)
    greet(me, CTX_ALL)
    mine = ctx_of(me)

    def columns(at):
        return pl.ds(pl.multiple_of(ctx_of(at) * HEAD_SIZE, HEAD_SIZE), HEAD_SIZE)

    copies = []
    for o in CTX_ALL:
        to = moved(me, o)
        copies.append(net.put(src.at[:, columns(to)], dst.at[mine], to))
    own = net.local(src.at[:, columns(me)], dst.at[mine])
    for copy in copies:
        copy.wait_recv()
    own.wait()
    net.finish()


def tokens_to_heads(grad_att):
    return remote(
        tokens_to_heads_body,
        "tokens_to_heads",
        4,
        shape((16, TOK, HEAD_SIZE), BF),
        [ANY],
        ANY,
        sems(16),
        grad_att,
    )


def ring_gather_body(src, dst, send, recv):
    me = place()
    z, c = me[0], me[4]
    net = Net(send, recv)
    greet(me, RING + [SIBLING])
    over = moved(me, SIBLING)
    copies = [net.put(src, dst.at[z, c], moved(me, o)) for o in RING]
    passed = [net.put(src, dst.at[z, c], over)]
    own = net.local(src, dst.at[z, c])
    for o, copy in zip(RING, copies):
        copy.wait_recv()
        s = before(me, o)[0]
        passed.append(net.put(dst.at[s, c], dst.at[s, c], over))
    for copy in passed:
        copy.wait_recv()
    own.wait()
    net.finish()


def ring_gather(second_in):
    return remote(
        ring_gather_body,
        "ring_gather",
        5,
        shape((4, 2, TOK, WIDTH), BF),
        [ANY],
        ANY,
        sems(16),
        second_in,
    )


def add_blocks(count, rows, first, second, out):
    @pl.loop(0, count)
    def _(k):
        @pl.loop(0, TOK // rows)
        def _(r):
            at = pl.ds(pl.multiple_of(r * rows, rows), rows)
            out[k, at] = (first[k, at].astype(F32) + second[k, at].astype(F32)).astype(BF)


def sum_blocks(count, rows, own, received, out):
    @pl.loop(0, TOK // rows)
    def _(r):
        at = pl.ds(pl.multiple_of(r * rows, rows), rows)
        total = own[at].astype(F32)
        for k in range(count):
            total = total + received[k, at].astype(F32)
        out[at] = total


def ring_scatter_body(parts, out, got, held, mixed, arrived, send, recv):
    me = place()
    z, c = me[0], me[4]
    net = Net(send, recv)
    greet(me, RING + [SIBLING])
    over = moved(me, SIBLING)
    first = net.put(parts.at[:, 1 - c], got, over)
    own = net.local(parts.at[:, c], held)
    own.wait()
    first.wait_recv()
    add_blocks(4, 32, held, got, mixed)
    copies = []
    for k, o in enumerate(RING):
        to = moved(me, o)
        copies.append(net.put(mixed.at[to[0]], arrived.at[k], to))
    for copy in copies:
        copy.wait_recv()
    sum_blocks(3, 32, mixed.at[z], arrived, out)
    net.finish()


def ring_scatter(parts):
    return remote(
        ring_scatter_body,
        "ring_scatter",
        6,
        shape((TOK, WIDTH), F32),
        [ANY],
        VMEM,
        [pltpu.VMEM((4, TOK, WIDTH), BF)] * 3 + [pltpu.VMEM((3, TOK, WIDTH), BF)] + sems(8),
        parts,
    )


def last_scatter_body(
    parts, dwq, gains, out, dwq_out, gain_out,
    got, held, mixed, arrived, dw_got, dw_sum, g_ctx, g_mine, g_dp, send, recv,
):
    me = place()
    xh, y, c = me[2], me[3], me[4]
    net = Net(send, recv)
    greet(me, CTX_ALL + DP_ALL)
    over = moved(me, SIBLING)
    mine, here = ctx_of(me), dp_of(me)
    first = net.put(parts.at[:, 1 - c], got, over)
    own = net.local(parts.at[:, c], held)
    columns = []
    for k, o in enumerate(DP_ALL):
        to = moved(me, o)
        columns.append(net.put(dwq.at[dp_of(to)], dw_got.at[k], to))
    small = [net.put(gains, g_ctx.at[k], moved(me, o)) for k, o in enumerate(CTX_ALL)]
    own.wait()
    first.wait_recv()
    add_blocks(8, 32, held, got, mixed)
    copies = []
    for k, o in enumerate(CTX_SAME):
        to = moved(me, o)
        copies.append(net.put(mixed.at[to[2] * 4 + to[3]], arrived.at[k], to))
    for copy in small:
        copy.wait_recv()
    total = gains[...]
    for k in range(15):
        total = total + g_ctx[k]
    g_mine[...] = total
    small = [net.put(g_mine, g_dp.at[k], moved(me, o)) for k, o in enumerate(DP_ALL)]
    for copy in columns:
        copy.wait_recv()
    dw = dwq[here].astype(F32)
    for k in range(7):
        dw = dw + dw_got[k].astype(F32)
    dw_sum[...] = dw.reshape(16, 8, 2 * HEAD_SIZE)
    rows = []
    for o in CTX_ALL:
        to = moved(me, o)
        rows.append(net.put(dw_sum.at[ctx_of(to)], dwq_out.at[mine], to))
    keep = net.local(dw_sum.at[mine], dwq_out.at[mine])
    for copy in small:
        copy.wait_recv()
    total = g_mine[...]
    for k in range(7):
        total = total + g_dp[k]
    gain_out[...] = total
    for copy in copies:
        copy.wait_recv()
    sum_blocks(7, 32, mixed.at[xh * 4 + y], arrived, out)
    for copy in rows:
        copy.wait_recv()
    keep.wait()
    net.finish()


def last_scatter(parts, dwq, gains):
    return remote(
        last_scatter_body,
        "last_scatter",
        7,
        (shape((TOK, WIDTH), F32), shape((16, 8, 2 * HEAD_SIZE), F32), shape((24, 128), F32)),
        [ANY, VMEM, VMEM],
        (VMEM, ANY, VMEM),
        [pltpu.VMEM((8, TOK, WIDTH), BF)] * 3
        + [
            pltpu.VMEM((7, TOK, WIDTH), BF),
            pltpu.VMEM((7, TOK, 2 * HEAD_SIZE), BF),
            pltpu.VMEM((16, 8, 2 * HEAD_SIZE), F32),
            pltpu.VMEM((15, 24, 128), F32),
            pltpu.VMEM((24, 128), F32),
            pltpu.VMEM((7, 24, 128), F32),
        ]
        + sems(72),
        parts,
        dwq,
        gains,
    )


def weight_scatter_body(
    dwo, dgu, dwd, parts, wo_out, gu_out, wd_out, out,
    wo_got, wo_one, wo_ring, wo_two, wo_plane, gu_got, gu_sum, wd_got, wd_sum, wd_half,
    p_got, p_one, p_ring, send, recv, gate,
):
    me = place()
    z, xl, xh, y, c = me
    net = Net(send, recv)
    barrier = pltpu.get_barrier_semaphore()
    peers = PLANE + RING_ALL
    for o in peers:
        pl.semaphore_signal(barrier, inc=1, device_id=moved(me, o), device_id_type=BY_MESH)
    for o in CTX_SAME:
        pl.semaphore_signal(barrier, inc=1, device_id=swapped(me, o), device_id_type=BY_MESH)

    @pl.when(xl != c)
    def _():
        pl.semaphore_signal(barrier, inc=1, device_id=(z, c, xh, y, xl), device_id_type=BY_MESH)

    pl.semaphore_wait(barrier, len(peers) + len(CTX_SAME) + (xl + c - 2 * xl * c))
    over = moved(me, SIBLING)
    near_wo = net.put(dwo.at[:, :, 1 - c], wo_got, over)
    near_p = net.put(parts.at[:, 1 - c], p_got, over)
    ups = []
    for k, o in enumerate(PLANE):
        to = moved(me, o)
        ups.append(net.put(dgu.at[:, plane_of(to)], gu_got.at[k], to))
    downs = []
    for k, o in enumerate(CTX_SAME):
        to = swapped(me, o)
        downs.append(net.put(dwd.at[to[2] * 4 + to[3]], wd_got.at[k + 1], to))

    @pl.when(xl != c)
    def _():
        copy = pltpu.make_async_remote_copy(
            src_ref=dwd.at[xh * 4 + y],
            dst_ref=wd_got.at[0],
            send_sem=gate.at[0],
            recv_sem=gate.at[1],
            device_id=(z, c, xh, y, xl),
            device_id_type=BY_MESH,
        )
        copy.start()
        copy.wait()

    @pl.when(xl == c)
    def _():
        copy = pltpu.make_async_copy(dwd.at[xh * 4 + y], wd_got.at[0], gate.at[0])
        copy.start()
        copy.wait()

    near_wo.wait_recv()

    @pl.loop(0, 4)
    def _(a):
        @pl.loop(0, 16)
        def _(b):
            wo_one[a, b] = (dwo[a, b, c].astype(F32) + wo_got[a, b].astype(F32)).astype(BF)

    ring = []
    for k, o in enumerate(RING):
        to = moved(me, o)
        ring.append(net.put(wo_one.at[to[0]], wo_ring.at[k], to))
    near_p.wait_recv()
    add_blocks(4, 32, parts.at[:, c], p_got, p_one)
    p_copies = []
    for k, o in enumerate(RING):
        to = moved(me, o)
        p_copies.append(net.put(p_one.at[to[0]], p_ring.at[k], to))
    for copy in ring:
        copy.wait_recv()

    @pl.loop(0, 16)
    def _(b):
        total = wo_one[z, b].astype(F32)
        for k in range(3):
            total = total + wo_ring[k, b].astype(F32)
        wo_two[b] = total.astype(BF)

    flat = []
    for k, o in enumerate(PLANE):
        to = moved(me, o)
        flat.append(net.put(wo_two.at[plane_of(to)], wo_plane.at[k], to))
    for copy in ups:
        copy.wait_recv()

    @pl.loop(0, 4)
    def _(a):
        total = dgu[a, plane_of(me)].astype(F32)
        for k in range(15):
            total = total + gu_got[k, a].astype(F32)
        gu_sum[2 * a] = total[:8]
        gu_sum[2 * a + 1] = total[8:]

    slices = []
    for o in RING_ALL:
        to = moved(me, o)
        slices.append(net.put(gu_sum.at[ring_of(to)], gu_out.at[ring_of(me)], to))
    keep = net.local(gu_sum.at[ring_of(me)], gu_out.at[ring_of(me)])
    for copy in downs:
        copy.wait_recv()
    total = wd_got[0].astype(F32)
    for k in range(1, 8):
        total = total + wd_got[k].astype(F32)
    wd_sum[0] = total[:24]
    wd_sum[1] = total[24:]
    half = net.put(wd_sum.at[1 - c], wd_half, over)
    for copy in p_copies:
        copy.wait_recv()
    sum_blocks(3, 32, p_one.at[z], p_ring, out)
    half.wait_recv()
    wd_out[...] = wd_sum[c] + wd_half[...]
    for copy in flat:
        copy.wait_recv()
    total = wo_two[plane_of(me)].astype(F32)
    for k in range(15):
        total = total + wo_plane[k].astype(F32)
    wo_out[...] = total
    for copy in slices:
        copy.wait_recv()
    keep.wait()
    net.finish()


def weight_scatter(dwo, dgu, dwd, parts):
    return remote(
        weight_scatter_body,
        "weight_scatter",
        8,
        (
            shape((16, WIDTH), F32),
            shape((8, 8, 2 * SLICE), F32),
            shape((24, WIDTH), F32),
            shape((TOK, WIDTH), F32),
        ),
        [VMEM] * 4,
        (VMEM, ANY, VMEM, VMEM),
        [
            pltpu.VMEM((4, 16, 16, WIDTH), BF),
            pltpu.VMEM((4, 16, 16, WIDTH), BF),
            pltpu.VMEM((3, 16, 16, WIDTH), BF),
            pltpu.VMEM((16, 16, WIDTH), BF),
            pltpu.VMEM((15, 16, WIDTH), BF),
            pltpu.VMEM((15, 4, 16, 2 * SLICE), BF),
            pltpu.VMEM((8, 8, 2 * SLICE), F32),
            pltpu.VMEM((8, 48, WIDTH), BF),
            pltpu.VMEM((2, 24, WIDTH), F32),
            pltpu.VMEM((24, WIDTH), F32),
            pltpu.VMEM((4, TOK, WIDTH), BF),
            pltpu.VMEM((4, TOK, WIDTH), BF),
            pltpu.VMEM((3, TOK, WIDTH), BF),
        ]
        + sems(72)
        + [pltpu.SemaphoreType.DMA((2,))],
        dwo,
        dgu,
        dwd,
        parts,
    )


def dot(a, b):
    return jnp.dot(a, b, preferred_element_type=F32)


def dot_t(a, b):
    return lax.dot_general(a, b, (((1,), (1,)), ((), ())), preferred_element_type=F32)


def t_dot(a, b):
    return lax.dot_general(a, b, (((0,), (0,)), ((), ())), preferred_element_type=F32)


def turned(v):
    half = HEAD_SIZE // 2
    return jnp.concatenate([-v[:, half:], v[:, :half]], 1)


def turned_back(v):
    half = HEAD_SIZE // 2
    return jnp.concatenate([v[:, half:], -v[:, :half]], 1)


def inverse_root(v):
    return lax.rsqrt(jnp.mean(v * v, -1, keepdims=True) + EPS)


def visible_at(begin, i, b):
    row = i * BLOCK + lax.broadcasted_iota(jnp.int32, (BLOCK, BLOCK), 0)
    col = b * BLOCK + lax.broadcasted_iota(jnp.int32, (BLOCK, BLOCK), 1)
    return (col >= begin) & (col <= row)


def attend_body(
    x, w, gain, q_gain, k_gain, cos, sin, begin,
    q_out, k_out, v_out, qu_out, ku_out, att_out, full_out, norm_out,
):
    i = pl.program_id(0)
    at = pl.ds(pl.multiple_of(i * BLOCK, BLOCK), BLOCK)
    inputs = x[...].astype(F32)
    first_in = (inputs * inverse_root(inputs) * gain[...]).astype(BF)
    projected = dot(first_in, w[...])
    q_un = projected[:, :HEAD_SIZE]
    k_un = projected[:, HEAD_SIZE : 2 * HEAD_SIZE]
    v_out[at] = projected[:, 2 * HEAD_SIZE :].astype(BF)
    qu_out[...] = q_un
    ku_out[...] = k_un
    cosine, sine = cos[...], sin[...]
    q_scaled = q_un * inverse_root(q_un) * q_gain[...]
    k_scaled = k_un * inverse_root(k_un) * k_gain[...]
    q = (q_scaled * cosine + turned(q_scaled) * sine).astype(BF)
    q_out[...] = q
    k_out[at] = (k_scaled * cosine + turned(k_scaled) * sine).astype(BF)
    start = begin[...]

    def step(b, carry):
        total, acc = carry
        cols = pl.ds(pl.multiple_of(b * BLOCK, BLOCK), BLOCK)
        s = dot_t(q, k_out[cols])
        e = jnp.where(visible_at(start, i, b), jnp.exp2(s * SCALE2), 0.0)
        total = total + jnp.sum(e, 1, keepdims=True)
        acc = acc + dot(e.astype(BF), v_out[cols])
        return total, acc

    total, acc = lax.fori_loop(
        0, i + 1, step, (jnp.zeros((BLOCK, 1), F32), jnp.zeros((BLOCK, HEAD_SIZE), F32))
    )
    norm = 1.0 / total
    full = acc * norm
    full_out[...] = full
    att_out[...] = full.astype(BF)
    norm_out[...] = jnp.broadcast_to(norm, (BLOCK, HEAD_SIZE))


def attend(x, w, gain, q_gain, k_gain, cos, sin, begin):
    rows = lambda cols: pl.BlockSpec((BLOCK, cols), lambda i: (i, 0))
    whole = lambda r, cols: pl.BlockSpec((r, cols), lambda i: (0, 0))
    head = (GROUP, HEAD_SIZE)
    return pl.pallas_call(
        attend_body,
        name="attend",
        grid=(GROUP // BLOCK,),
        in_specs=[
            rows(WIDTH),
            whole(WIDTH, 3 * HEAD_SIZE),
            whole(1, WIDTH),
            whole(1, HEAD_SIZE),
            whole(1, HEAD_SIZE),
            rows(HEAD_SIZE),
            rows(HEAD_SIZE),
            rows(1),
        ],
        out_specs=(
            rows(HEAD_SIZE),
            whole(*head),
            whole(*head),
            rows(HEAD_SIZE),
            rows(HEAD_SIZE),
            rows(HEAD_SIZE),
            rows(HEAD_SIZE),
            rows(HEAD_SIZE),
        ),
        out_shape=(
            shape(head, BF),
            shape(head, BF),
            shape(head, BF),
            shape(head, F32),
            shape(head, F32),
            shape(head, BF),
            shape(head, F32),
            shape(head, F32),
        ),
        compiler_params=pltpu.CompilerParams(vmem_limit_bytes=50 * MIB),
    )(x, w, gain, q_gain, k_gain, cos, sin, begin)


def attend_back_body(q, k, v, grad, full, norm, begin, dq_out, dk_out, dv_out):
    i = pl.program_id(0)

    @pl.when(i == 0)
    def _():
        dk_out[...] = jnp.zeros_like(dk_out)
        dv_out[...] = jnp.zeros_like(dv_out)

    qb, gb = q[...], grad[...]
    inverse = norm[...][:, :1]
    inner = jnp.sum(gb.astype(F32) * full[...], 1, keepdims=True)
    start = begin[...]

    def step(b, acc):
        cols = pl.ds(pl.multiple_of(b * BLOCK, BLOCK), BLOCK)
        kb, vb = k[cols], v[cols]
        s = dot_t(qb, kb)
        p = jnp.where(visible_at(start, i, b), jnp.exp2(s * SCALE2) * inverse, 0.0)
        dp = dot_t(gb, vb)
        ds = (p * (dp - inner)).astype(BF)
        dv_out[cols] += t_dot(p.astype(BF), gb)
        dk_out[cols] += t_dot(ds, qb)
        return acc + dot(ds, kb)

    dq_out[...] = lax.fori_loop(0, i + 1, step, jnp.zeros((BLOCK, HEAD_SIZE), F32)) * SCALE

    @pl.when(i == GROUP // BLOCK - 1)
    def _():
        dk_out[...] = dk_out[...] * SCALE


def attend_back(q, k, v, grad, full, norm, begin):
    rows = lambda cols: pl.BlockSpec((BLOCK, cols), lambda i: (i, 0))
    whole = lambda r, cols: pl.BlockSpec((r, cols), lambda i: (0, 0))
    head = (GROUP, HEAD_SIZE)
    return pl.pallas_call(
        attend_back_body,
        name="attend_back",
        grid=(GROUP // BLOCK,),
        in_specs=[rows(HEAD_SIZE), whole(*head), whole(*head)] + [rows(HEAD_SIZE)] * 3 + [rows(1)],
        out_specs=(rows(HEAD_SIZE), whole(*head), whole(*head)),
        out_shape=(shape(head, F32),) * 3,
        compiler_params=pltpu.CompilerParams(vmem_limit_bytes=50 * MIB),
    )(q, k, v, grad, full, norm, begin)


def feed_forward_body(s_in, cot, w_gu, w_d, p_out, p_grad, dgu_out, dwd_out, dgu_acc, dwd_acc):
    i = pl.program_id(0)

    @pl.when(i == 0)
    def _():
        dgu_acc[...] = jnp.zeros_like(dgu_acc)
        dwd_acc[...] = jnp.zeros_like(dwd_acc)

    s, ct = s_in[...], cot[...]
    gu = dot(s, w_gu[...])
    gate, up = gu[:, :SLICE], gu[:, SLICE:]
    sigma = 1.0 / (1.0 + jnp.exp(-gate))
    swish = gate * sigma
    hidden = (swish * up).astype(BF)
    p_out[...] = dot(hidden, w_d[...]).astype(BF)
    grad_hidden = dot_t(ct, w_d[...])
    grad_gate = grad_hidden * up * sigma * (1.0 + gate * (1.0 - sigma))
    grad_gu = jnp.concatenate([grad_gate, grad_hidden * swish], 1).astype(BF)
    p_grad[...] = dot_t(grad_gu, w_gu[...]).astype(BF)
    dgu_acc[...] += t_dot(s, grad_gu)
    dwd_acc[...] += t_dot(hidden, ct)

    @pl.when(i == pl.num_programs(0) - 1)
    def _():
        dgu_out[...] = dgu_acc[...].astype(BF)
        dwd_out[...] = dwd_acc[...].astype(BF)


def feed_forward(s_in, cot, w_gu, w_d):
    rows = pl.BlockSpec((BLOCK, WIDTH), lambda i: (i, 0))
    whole = lambda r, cols: pl.BlockSpec((r, cols), lambda i: (0, 0))
    return pl.pallas_call(
        feed_forward_body,
        name="feed_forward",
        grid=(8 * TOK // BLOCK,),
        in_specs=[rows, rows, whole(WIDTH, 2 * SLICE), whole(SLICE, WIDTH)],
        out_specs=(rows, rows, whole(WIDTH, 2 * SLICE), whole(SLICE, WIDTH)),
        out_shape=(
            shape((8 * TOK, WIDTH), BF),
            shape((8 * TOK, WIDTH), BF),
            shape((WIDTH, 2 * SLICE), BF),
            shape((SLICE, WIDTH), BF),
        ),
        scratch_shapes=[pltpu.VMEM((WIDTH, 2 * SLICE), F32), pltpu.VMEM((SLICE, WIDTH), F32)],
        compiler_params=pltpu.CompilerParams(vmem_limit_bytes=50 * MIB),
    )(s_in, cot, w_gu, w_d)


def head_back(unnormed, grad, cosine, sine, gain):
    inverse = inverse_root(unnormed)
    hat = unnormed * inverse
    back = grad * cosine + turned_back(grad * sine)
    g = back * gain
    raw = inverse * (g - hat * jnp.mean(g * hat, -1, keepdims=True))
    return raw, jnp.sum(back * hat, 0, keepdims=True)


def project_back_body(
    x, w, gain, q_gain, k_gain, cos, sin, q_un, k_un, dq, dkv, got, flag,
    parts, dw_out, gains_out, q_gain_out, k_gain_out, dw_acc,
):
    i = pl.program_id(0)

    @pl.when(i == 0)
    def _():
        dw_acc[...] = jnp.zeros_like(dw_acc)
        gains_out[...] = jnp.zeros_like(gains_out)
        q_gain_out[...] = jnp.zeros_like(q_gain_out)
        k_gain_out[...] = jnp.zeros_like(k_gain_out)

    is_key = flag[...]
    inputs = x[...].astype(F32)
    normed = inputs * inverse_root(inputs)
    first_in = (normed * gain[...]).astype(BF)
    cosine, sine = cos[...], sin[...]
    dq_raw, q_part = head_back(q_un[...], dq[...], cosine, sine, q_gain[...])
    both = dkv[...] + got[...].astype(F32)
    dk_raw, k_part = head_back(k_un[...], both, cosine, sine, k_gain[...])
    second = jnp.where(is_key > 0.5, dk_raw, both)
    grad = jnp.concatenate([dq_raw, second], 1).astype(BF)
    dw_acc[...] += t_dot(first_in, grad)
    grad_first = dot_t(grad, w[...])
    parts[...] = grad_first.astype(BF)
    gains_out[...] += jnp.sum(grad_first * normed, 0, keepdims=True)
    q_gain_out[...] += q_part
    k_gain_out[...] += k_part * is_key

    @pl.when(i == pl.num_programs(0) - 1)
    def _():
        dw_out[...] = dw_acc[...].astype(BF)


def project_back(x, w, gain, q_gain, k_gain, cos, sin, q_un, k_un, dq, dkv, got, flag):
    rows = lambda cols: pl.BlockSpec((BLOCK, cols), lambda i: (i, 0))
    whole = lambda r, cols: pl.BlockSpec((r, cols), lambda i: (0, 0))
    return pl.pallas_call(
        project_back_body,
        name="project_back",
        grid=(GROUP // BLOCK,),
        in_specs=[
            rows(WIDTH),
            whole(WIDTH, 2 * HEAD_SIZE),
            whole(1, WIDTH),
            whole(1, HEAD_SIZE),
            whole(1, HEAD_SIZE),
        ]
        + [rows(HEAD_SIZE)] * 7
        + [whole(1, HEAD_SIZE)],
        out_specs=(
            rows(WIDTH),
            whole(WIDTH, 2 * HEAD_SIZE),
            whole(1, WIDTH),
            whole(1, HEAD_SIZE),
            whole(1, HEAD_SIZE),
        ),
        out_shape=(
            shape((GROUP, WIDTH), BF),
            shape((WIDTH, 2 * HEAD_SIZE), BF),
            shape((1, WIDTH), F32),
            shape((1, HEAD_SIZE), F32),
            shape((1, HEAD_SIZE), F32),
        ),
        scratch_shapes=[pltpu.VMEM((WIDTH, 2 * HEAD_SIZE), F32)],
        compiler_params=pltpu.CompilerParams(vmem_limit_bytes=50 * MIB),
    )(x, w, gain, q_gain, k_gain, cos, sin, q_un, k_un, dq, dkv, got, flag)


def swap_body(src, dst, send, recv):
    me = place()
    net = Net(send, recv)
    greet(me, [SIBLING])
    net.put(src, dst, moved(me, SIBLING)).wait_recv()
    net.finish()


def swap(values):
    return remote(
        swap_body, "swap", 9, shape(values.shape, values.dtype), [ANY], ANY, sems(1), values
    )


def layout(doc_lengths):
    ends = jnp.cumsum(doc_lengths)
    index = jnp.arange(GROUP, dtype=jnp.int32)
    starts = ends - doc_lengths
    begin = jnp.max(jnp.where(index[:, None] >= starts[None, :], starts[None, :], 0), 1)
    return begin, index - begin


def angles(position):
    half = HEAD_SIZE // 2
    freq = THETA ** (-(jnp.arange(half, dtype=F32) * 2.0 / HEAD_SIZE))
    phase = position.astype(F32)[:, None] * freq[None, :]
    cosine, sine = jnp.cos(phase), jnp.sin(phase)
    return jnp.concatenate([cosine, cosine], 1), jnp.concatenate([sine, sine], 1)


def norm_back(values, inverse, grad):
    cubed = inverse * inverse * inverse
    return inverse * grad - values * cubed * jnp.mean(grad * values, -1, keepdims=True)


def on_device(
    tokens, lengths, attn_gain, q_gain, k_gain, qkv, w_out, mlp_gain, w_gate_up, w_down, cotangent
):
    core = lax.axis_index("c")
    device = lax.axis_index(AXES)
    key_at, value_at = QUERY_HEADS * HEAD_SIZE, (QUERY_HEADS + KEY_VALUE_HEADS) * HEAD_SIZE

    rows = qkv.astype(F32)
    wq = rows[:, :key_at].reshape(8, 16, 1, HEAD_SIZE)
    wk = jnp.repeat(rows[:, key_at:value_at].reshape(8, 8, 1, HEAD_SIZE), 2, axis=1)
    wv = jnp.repeat(rows[:, value_at:].reshape(8, 8, 1, HEAD_SIZE), 2, axis=1)
    wq = jnp.concatenate([wq, wk, wv], 2).reshape(8, 16, 3 * HEAD_SIZE).swapaxes(0, 1)
    gains = jnp.concatenate([attn_gain, mlp_gain, q_gain, k_gain]).astype(F32)
    gains = jnp.broadcast_to(jnp.pad(gains, (0, 128 - 18))[None], (8, 128))
    begin, position = layout(lengths[0])
    begin = begin[:, None]
    cosine, sine = angles(position)

    x_all, w_qkv, gains = first_gather(tokens, wq, gains)
    x_all = x_all.reshape(GROUP, WIDTH)
    w_qkv = w_qkv.reshape(WIDTH, 3 * HEAD_SIZE)
    gains = gains.reshape(128, 128)
    gain_one = gains[:, :8].reshape(1, WIDTH)
    gain_two = gains[:, 8:16].reshape(1, WIDTH)
    gain_q = gains[:, 16].reshape(1, HEAD_SIZE)
    gain_k = gains[:, 17].reshape(1, HEAD_SIZE)

    q, k, v, q_un, k_un, att, full, norm = attend(
        x_all, w_qkv, gain_one, gain_q, gain_k, cosine, sine, begin
    )
    attended = heads_to_tokens(att)

    wgu = w_gate_up.astype(F32)
    wgu = jnp.concatenate(
        [wgu[:, :FF].reshape(8, 8, SLICE), wgu[:, FF:].reshape(8, 8, SLICE)], 2
    ).swapaxes(0, 1)
    wo_all, gu_all, wd_all, cot_all = weight_gather(w_out, wgu, w_down.astype(F32), cotangent)
    wo_all = wo_all.reshape(QUERY_HEADS * HEAD_SIZE, WIDTH)
    gu_all = gu_all.reshape(WIDTH, 2 * SLICE)
    wd_all = wd_all.reshape(SLICE, WIDTH)
    cot_all = cot_all.reshape(8 * TOK, WIDTH)

    inputs = tokens.astype(F32)
    residual = inputs + dot(attended, wo_all)
    inverse_two = inverse_root(residual)
    second_in = (residual * inverse_two * gain_two).astype(BF)
    s_all = ring_gather(second_in).reshape(8 * TOK, WIDTH)
    p_out, p_grad, dgu, dwd = feed_forward(s_all, cot_all, gu_all, wd_all)
    grad_second = ring_scatter(p_grad.reshape(4, 2, TOK, WIDTH))

    grad_gain_two = jnp.sum(grad_second * (residual * inverse_two), 0)
    grad_resid = cotangent.astype(F32) + norm_back(residual, inverse_two, grad_second * gain_two)
    resid_low = grad_resid.astype(BF)
    grad_att = dot_t(resid_low, wo_all).astype(BF)
    dwo = t_dot(attended, resid_low).astype(BF)
    grad_heads = tokens_to_heads(grad_att).reshape(GROUP, HEAD_SIZE)

    dq, dk, dv = attend_back(q, k, v, grad_heads, full, norm, begin)
    is_key = core == 0
    dkv = jnp.where(is_key, dk, dv)
    got = swap(jnp.where(is_key, dv, dk).astype(BF))
    flag = jnp.broadcast_to(is_key.astype(F32), (1, HEAD_SIZE))
    w_two = jnp.concatenate(
        [
            w_qkv[:, :HEAD_SIZE],
            jnp.where(is_key, w_qkv[:, HEAD_SIZE : 2 * HEAD_SIZE], w_qkv[:, 2 * HEAD_SIZE :]),
        ],
        1,
    )
    parts, dwq, grad_gain_one, grad_gain_q, grad_gain_k = project_back(
        x_all, w_two, gain_one, gain_q, gain_k, cosine, sine, q_un, k_un, dq, dkv, got, flag
    )
    packed = jnp.concatenate(
        [
            grad_gain_one.reshape(8, 128),
            grad_gain_two.reshape(8, 128),
            grad_gain_q,
            grad_gain_k,
            jnp.zeros((6, 128), F32),
        ]
    )
    grad_first, dwq, packed = last_scatter(
        parts.reshape(8, 2, TOK, WIDTH), dwq.reshape(8, TOK, 2 * HEAD_SIZE), packed
    )
    inverse_one = inverse_root(inputs)
    input_grad = grad_resid + norm_back(inputs, inverse_one, grad_first * gain_one)

    grad_w_out, dgu, grad_down, mlp_out = weight_scatter(
        dwo.reshape(4, 16, 2, 16, WIDTH),
        dgu.reshape(4, 16, 16, 2 * SLICE),
        dwd.reshape(8, 48, WIDTH),
        p_out.reshape(4, 2, TOK, WIDTH),
    )
    output = residual + mlp_out

    dwq = dwq.swapaxes(0, 1)
    dkv_cols = dwq[:, :, HEAD_SIZE:].reshape(8, 8, 2, HEAD_SIZE)
    grad_w_qkv = jnp.concatenate(
        [
            dwq[:, :, :HEAD_SIZE].reshape(8, -1),
            dkv_cols[:, :, 0].reshape(8, -1),
            dkv_cols[:, :, 1].reshape(8, -1),
        ],
        1,
    )
    dgu = dgu.swapaxes(0, 1)
    grad_gate_up = jnp.concatenate(
        [dgu[:, :, :SLICE].reshape(8, FF), dgu[:, :, SLICE:].reshape(8, FF)], 1
    )

    def own(first, rows, each):
        return lax.dynamic_slice_in_dim(packed[first : first + rows].reshape(-1), device * each, each)

    return (
        output,
        input_grad,
        own(0, 8, 8),
        own(16, 1, 1),
        own(17, 1, 1),
        grad_w_qkv,
        grad_w_out,
        own(8, 8, 8),
        grad_gate_up,
        grad_down,
    )


def solution(mesh):
    torus = Mesh(mesh.devices.reshape(SIZES), AXES)
    rows, line = P(AXES, None), P(AXES)
    return jax.shard_map(
        on_device,
        mesh=torus,
        in_specs=(rows, P(DP, None), line, line, line, rows, rows, line, rows, rows, rows),
        out_specs=(rows, rows, line, line, line, rows, rows, line, rows, rows),
        check_vma=False,
    )
```

time: 2130 us -> 372 us (0.17)
  waiting for transfers between devices: 1600 us -> 0 us
  Pallas kernels: 0 us -> 330 us
  local copies, waits for them, and re-layouts: 327 us -> 12.3 us
  matrix products: 122 us -> 8.32 us
  other arithmetic: 47.5 us -> 17.8 us
    reduce_scatter x4 -> x0, waiting for transfers between devices: 1130 us -> none  [the longest x1 675 us: scatter_lines(): own = lax.psum_scatter(lines, axis, scatter_dimension=0, tiled=True)]
    unnamed x9 -> x0, waiting for transfers between devices: 470 us -> none
    pallas_call x0 -> x13, Pallas kernels: none -> 330 us  [the longest x9 259 us: remote(): pl.pallas_call(body, name=name, out_shape=outs, in_specs=ins, out_specs=o...]
    dot_general x18 -> x3, matrix products: 122 us -> 8.32 us  [the longest x1 3.57 us: dot(): return jnp.dot(a, b, preferred_element_type=F32)]
    another operation x8 -> x1, local copies, waits for them, and re-layouts: 76.9 us -> 0.01 us  [on_device(): dkv_cols[:, :, 0].reshape(8, -1)]
    all_gather x2 -> x0, local copies, waits for them, and re-layouts: 75.9 us -> none  [gather_packed(): lines, at, finished = (lax.all_gather(ravelled, axis), 0, [])]
    reshape x12 -> x5, local copies, waits for them, and re-layouts: 54.4 us -> 0.12 us  [the longest x1 0.1 us: on_device(): gain_one = gains[:, :8].reshape(1, WIDTH)]
    unnamed x107 -> x36, local copies, waits for them, and re-layouts: 49.9 us -> 7.08 us
  transfers between devices with their start and end apart: 7 -> 0, of which waited for: 5 -> 0; matrix products, arithmetic and copies ran while one was open for 15% -> 0% of each run, Pallas kernels for 0% -> 0%
where the time goes in v1:
time: 372 us; the launch traced here: 371 us
  Pallas kernels  330 us (89%)
  other arithmetic  17.8 us (5%)
  local copies, waits for them, and re-layouts  12.3 us (3%)
  matrix products  8.32 us (2%)
    pallas_call x9, Pallas kernels, remote(): pl.pallas_call(body, name=name, out_shape=outs, in_specs=ins, out_specs=o...  259 us
    pallas_call x1, Pallas kernels, attend_back(): pl.pallas_call(attend_back_body, name='attend_back', grid=(GROUP // BLOCK...  22.4 us
    pallas_call x1, Pallas kernels, attend(): pl.pallas_call(attend_body, name='attend', grid=(GROUP // BLOCK,), in_spe...  21.5 us
    pallas_call x1, Pallas kernels, project_back(): pl.pallas_call(project_back_body, name='project_back', grid=(GROUP // BLO...  13.8 us
    pallas_call x1, Pallas kernels, feed_forward(): pl.pallas_call(feed_forward_body, name='feed_forward', grid=(8 * TOK // B...  13.5 us

profile of v1, /device:TPU:0, one launch (start us, length us, event | category | flops | bytes accessed | tf_op | source)
XLA Modules:
  0.0 370.9 jit_solution(15878821293107941121)
XLA Ops:
  2.0 0.8 fusion.7
  2.7 0.8 reduce-window_clone.1
  3.6 0.7 subtract_bitcast_fusion
  4.2 0.1 select_reduce_fusion
  4.4 0.8 convert_element_type.47.wd
  5.2 0.8 convert_element_type.44
  6.1 0.9 fusion.10
  7.0 1.3 copy.31.begin
  8.4 3.7 multiply_sine_fusion
  12.0 1.9 pad_maximum_fusion
  14.0 45.4 %first_gather.1 = (bf16[16,128,1024]{2,1,0:T(8,128)(2,1)}, bf16[8,128,384]{2,1,0:T(8,128)(2,1)S(1)}, f32[8,16,128]{2,1,0:T(8,128)S(1)}) custom-call(bf16[128,1024]{1,0:T(8,128)(2,1)S(1)} %copy-done.3, f32[16,8,384]{2,1,0:T(8,128)S(1)} %maximum_bitcast_fusion.wq, f32[8,128]{1,0:T(8,128)S(1)} %broadcast_in_dim.46.gains), custom_call_target="tpu_custom_call" | custom-call | tf_op jit(solution)/shard_map/first_gather/pallas_call | solution.py:125
  59.4 0.2 slice_reduce_fusion
  60.1 21.5 %attend.1 = (bf16[2048,128]{1,0:T(8,128)(2,1)S(1)}, bf16[2048,128]{1,0:T(8,128)(2,1)S(1)}, bf16[2048,128]{1,0:T(8,128)(2,1)S(1)}, f32[2048,128]{1,0:T(8,128)S(1)...) custom-call(bf16[2048,1024]{1,0:T(8,128)(2,1)} %bitcast.86, ...), custom_call_target="tpu_custom_call" | custom-call | tf_op jit(solution)/shard_map/attend/pallas_call | solution.py:790
  81.6 1.0 copy-done.7
  82.6 11.2 %heads_to_tokens.1 = bf16[128,2048]{1,0:T(8,128)(2,1)S(1)} custom-call(bf16[16,128,128]{2,1,0:T(8,128)(2,1)S(1)} %bitcast.74), custom_call_target="tpu_custom_call" | custom-call | tf_op jit(solution)/shard_map/heads_to_tokens/pallas_call | solution.py:125
  93.9 47.8 %weight_gather.1 = (bf16[4,2,2,4,2,16,1024]{6,5,4,3,2,1,0:T(8,128)(2,1)}, bf16[4,2,2,4,16,768]{5,4,3,2,1,0:T(8,128)(2,1)S(1)}, bf16[2,4,48,1024]{3,2,1,0:T(8,128)(2,1)S(1)}, bf16[4,2,128,1024]{3,2,1,0:T(8,128)(2,1)}) custom-call(bf16[16,1024]{1,0:T(8,128)(2,1)S(1)} %copy-done.11, f32[8,8,768]{2,1,0:T(8,128)S(1)} %maximum_bitcast_fusion.1.wgu, ...), custom_call_target="tpu_custom_call" | custom-call | tf_op jit(solution)/shard_map/weight_gather/pallas_call | solution.py:125
  141.7 3.6 multiply_reduce_fusion.2
  145.3 0.1 multiply_convert_fusion.src
  145.4 17.3 %ring_gather.1 = bf16[4,2,128,1024]{3,2,1,0:T(8,128)(2,1)S(1)} custom-call(bf16[128,1024]{1,0:T(8,128)(2,1)S(1)} %multiply_convert_fusion.src), custom_call_target="tpu_custom_call" | custom-call | tf_op jit(solution)/shard_map/ring_gather/pallas_call | solution.py:125
  162.8 1.3 copy-done.2
  164.1 13.5 %feed_forward.1 = (bf16[1024,1024]{1,0:T(8,128)(2,1)}, bf16[1024,1024]{1,0:T(8,128)(2,1)}, bf16[1024,768]{1,0:T(8,128)(2,1)S(1)}, bf16[384,1024]{1,0:T(8,128)(2,1)S(1)}) custom-call(bf16[1024,1024]{1,0:T(8,128)(2,1)} %bitcast.63, bf16[1024,1024]{1,0:T(8,128)(2,1)} %bitcast.89, bf16[1024,768]{1,0:T(8,128)(2,1)} %bitcast.68, bf16[384,1024]{1,0:T(8,128)(2,1)S(1)} %bitcast.73), custom_call_target="tpu_custom_call" | custom-call | tf_op jit(solution)/shard_map/feed_forward/pallas_call | solution.py:905
  177.6 1.6 copy-done.4
  179.2 18.9 %ring_scatter.1 = f32[128,1024]{1,0:T(8,128)S(1)} custom-call(bf16[4,2,128,1024]{3,2,1,0:T(8,128)(2,1)S(1)} %bitcast.66), custom_call_target="tpu_custom_call" | custom-call | tf_op jit(solution)/shard_map/ring_scatter/pallas_call | solution.py:125
  198.1 0.2 multiply_reduce_fusion
  198.3 0.2 subtract_add_fusion
  198.5 1.5 convolution_convert_fusion.1.src
  200.1 12.0 %tokens_to_heads.1 = bf16[16,128,128]{2,1,0:T(8,128)(2,1)S(1)} custom-call(bf16[128,2048]{1,0:T(8,128)(2,1)S(1)} %convolution_convert_fusion.1.src), custom_call_target="tpu_custom_call" | custom-call | tf_op jit(solution)/shard_map/tokens_to_heads/pallas_call | solution.py:125
  212.0 22.4 %attend_back.1 = (f32[2048,128]{1,0:T(8,128)S(1)}, f32[2048,128]{1,0:T(8,128)}, f32[2048,128]{1,0:T(8,128)}) custom-call(bf16[2048,128]{1,0:T(8,128)(2,1)S(1)} %get-tuple-element.59.q, bf16[2048,128]{1,0:T(8,128)(2,1)S(1)} %get-tuple-element.60.k, bf16[2048,128]{1,0:T(8,128)(2,1)S(1)} %get-tuple-element.61.v, bf16[2048,128]{1,0:T(8,128)(2,1)S(1)} %bitcast.67, ...), custom_call_target="tpu_custom_call" | custom-call | tf_op jit(solution)/shard_map/attend_back/pallas_call | solution.py:863
  234.5 1.8 select_convert_fusion.src
  236.3 2.3 broadcast_select_fusion.dkv
  238.6 1.9 swap.1.got
  240.6 13.8 %project_back.1 = (bf16[2048,1024]{1,0:T(8,128)(2,1)}, bf16[1024,256]{1,0:T(8,128)(2,1)S(1)}, f32[1,1024]{1,0:T(1,128)S(1)}, f32[1,128]{1,0:T(1,128)S(1)}, f32[1,128]{1,0:T(1,128)S(1)}) custom-call(bf16[2048,1024]{1,0:T(8,128)(2,1)} %bitcast.87, bf16[1024,256]{1,0:T(8,128)(2,1)S(1)} %pad_maximum_fusion.2.w, f32[1,1024]{1,0:T(1,128)S(1)} %reshape.198.gain, ...), custom_call_target="tpu_custom_call" | custom-call | tf_op jit(solution)/shard_map/project_back/pallas_call | solution.py:969
  254.4 0.8 copy-done.9
  255.2 1.0 copy-done.10
  256.2 43.4 %last_scatter.1 = (f32[128,1024]{1,0:T(8,128)S(1)}, f32[16,8,256]{2,1,0:T(8,128)S(1)}, f32[24,128]{1,0:T(8,128)S(1)}) custom-call(bf16[8,2,128,1024]{3,2,1,0:T(8,128)(2,1)} %bitcast.88, bf16[8,128,256]{2,1,0:T(8,128)(2,1)S(1)} %bitcast.75, f32[24,128]{1,0:T(8,128)S(1)} %concatenate.33.gains), custom_call_target="tpu_custom_call" | custom-call | tf_op jit(solution)/shard_map/last_scatter/pallas_call | solution.py:125
  299.6 0.7 pad_maximum_fusion.4
  300.3 0.2 fusion
  300.5 1.0 fusion.3
  301.5 0.6 dynamic_slice.21
  302.1 0.6 dynamic_slice.16
  302.7 0.6 constant_dynamic-slice_fusion.1
  303.3 0.6 constant_dynamic-slice_fusion
  303.9 3.2 convolution_convert_fusion
  307.1 61.0 %weight_scatter.1 = (f32[16,1024]{1,0:T(8,128)S(1)}, f32[8,8,768]{2,1,0:T(8,128)S(1)}, f32[24,1024]{1,0:T(8,128)S(1)}, f32[128,1024]{1,0:T(8,128)S(1)}) custom-call(bf16[4,16,2,16,1024]{4,3,2,1,0:T(8,128)(2,1)} %bitcast.83, bf16[4,16,16,768]{3,2,1,0:T(8,128)(2,1)S(1)} %bitcast.69, bf16[8,48,1024]{2,1,0:T(8,128)(2,1)S(1)} %bitcast.72, ...), custom_call_target="tpu_custom_call" | custom-call | tf_op jit(solution)/shard_map/weight_scatter/pallas_call | solution.py:125
  368.1 0.9 add.59
  369.0 0.7 pad_maximum_fusion.3
  369.7 0.6 copy.37
  370.3 0.6 copy.38
  (56 shorter events, 0.7 us)
Async XLA Ops:
  6.1 7.9 %copy-start.3 = (bf16[128,1024]{1,0:T(8,128)(2,1)S(1)}, bf16[128,1024]{1,0:T(8,128)(2,1)}, u32[]{:S(2)}) copy-start(bf16[128,1024]{1,0:T(8,128)(2,1)} %tok.1) | copy-start | bytes 786436
  60.1 33.7 %copy-start.6 = (bf16[128,1024]{1,0:T(8,128)(2,1)S(1)}, bf16[128,1024]{1,0:T(8,128)(2,1)}, u32[]{:S(2)}) copy-start(bf16[128,1024]{1,0:T(8,128)(2,1)} %cot.1) | copy-start | bytes 786436
  60.1 33.7 %copy-start.11 = (bf16[16,1024]{1,0:T(8,128)(2,1)S(1)}, bf16[16,1024]{1,0:T(8,128)(2,1)}, u32[]{:S(2)}) copy-start(bf16[16,1024]{1,0:T(8,128)(2,1)} %wo.1) | copy-start | bytes 98308
  81.6 1.0 copy-start.7
  141.7 3.6 copy-start.5
  145.3 53.0 %copy-start.13 = (f32[128,1024]{1,0:T(8,128)}, f32[128,1024]{1,0:T(8,128)S(1)}, u32[]{:S(2)}) copy-start(f32[128,1024]{1,0:T(8,128)S(1)} %get-tuple-element.109) | copy-start | bytes 1572868
  162.7 1.3 copy-start.2
  164.1 34.4 %copy-start.12 = (bf16[4,2,2,4,2,16,1024]{6,5,4,3,2,1,0:T(8,128)(2,1)S(1)}, bf16[4,2,2,4,2,16,1024]{6,5,4,3,2,1,0:T(8,128)(2,1)}, u32[]{:S(2)}) copy-start(bf16[4,2,2,4,2,16,1024]{6,5,4,3,2,1,0:T(8,128)(2,1)} %get-tuple-element.48) | copy-start | bytes 12582916
  177.6 1.6 copy-start.4
  198.5 13.5 %copy-start.15 = (f32[128,1024]{1,0:T(8,128)}, f32[128,1024]{1,0:T(8,128)S(1)}, u32[]{:S(2)}) copy-start(f32[128,1024]{1,0:T(8,128)S(1)} %subtract_add_fusion) | copy-start | bytes 1572868
  234.5 6.1 %copy-start.8 = (f32[2048,128]{1,0:T(8,128)}, f32[2048,128]{1,0:T(8,128)S(1)}, u32[]{:S(2)}) copy-start(f32[2048,128]{1,0:T(8,128)S(1)} %get-tuple-element.64.dq) | copy-start | bytes 3145732
  234.5 6.1 %copy-start = (f32[2048,128]{1,0:T(8,128)S(1)}, f32[2048,128]{1,0:T(8,128)}, u32[]{:S(2)}) copy-start(f32[2048,128]{1,0:T(8,128)} %get-tuple-element.110.cos) | copy-start | bytes 3145732
  234.5 6.1 %copy-start.1 = (f32[2048,128]{1,0:T(8,128)S(1)}, f32[2048,128]{1,0:T(8,128)}, u32[]{:S(2)}) copy-start(f32[2048,128]{1,0:T(8,128)} %get-tuple-element.111.sin) | copy-start | bytes 3145732
  254.4 0.8 copy-start.9
  255.2 1.0 copy-start.10
  256.2 44.3 %copy-start.16 = (f32[128,1024]{1,0:T(8,128)S(1)}, f32[128,1024]{1,0:T(8,128)}, u32[]{:S(2)}) copy-start(f32[128,1024]{1,0:T(8,128)} %copy-done.15) | copy-start | bytes 1572868
  307.1 61.0 %copy-start.14 = (f32[128,1024]{1,0:T(8,128)S(1)}, f32[128,1024]{1,0:T(8,128)}, u32[]{:S(2)}) copy-start(f32[128,1024]{1,0:T(8,128)} %copy-done.13) | copy-start | bytes 1572868
